TPU v7x, 256 devices: a whole 4x4x8 slice. The times are simulated.
256 devices in a mesh: section: 8 (over z_lo, y), fsdp: 32 (over z_hi, x, core).
Axes of the slice: x: 4, y: 4, z: 8 (z_hi: 4, z_lo: 2; z = z_hi * 2 + z_lo), core: 2. Of those that a mesh axis runs over, the one named last changes fastest.
Arguments:
- hidden: bfloat16 [16384, 7168], P('fsdp', 'section'), may hold values from -600 to 600
- token_ids: int32 [16384], P('fsdp'), may hold values from 0 to 65535
- table: bfloat16 [7168, 65536], P(('section', 'fsdp')), may hold values from -600 to 600
- gain_hidden: float32 [7168], replicated, may hold values from 0.1 to 1.9
- gain_embed: float32 [7168], replicated, may hold values from 0.1 to 1.9
- proj_hidden: bfloat16 [7168, 4096], P(('section', 'fsdp')), may hold values from -0.046875 to 0.046875
- proj_embed: bfloat16 [7168, 4096], P(('section', 'fsdp')), may hold values from -0.046875 to 0.046875
Outputs:
- mixed: bfloat16 [16384, 4096], P('fsdp', 'section')
All inputs are finite; a program needn't handle non-finite values.
Results may differ from a plain program's by a relative error of at most 0.0049.
Values may be sent and summed in bfloat16 or wider, within the bound.
No kernel may reach another device: no remote copies, remote signals or barrier semaphores. Data moves between devices by JAX's collectives and lax.ppermute only.
A program may use at most 128 MiB of HBM per device.

v0:
```python
import jax
import jax.numpy as jnp
from jax import lax
from jax.sharding import PartitionSpec as P

EPS = 1e-06


def on_device(hidden, token_ids, table, gain_hidden, gain_embed, proj_hidden, proj_embed):
    model_width = gain_hidden.shape[0]
    block_width = hidden.shape[1]
    tokens_here = hidden.shape[0]
    shard_rows = proj_hidden.shape[0]
    sections = lax.axis_size("section")
    groups = lax.axis_size("fsdp")
    section_pos = lax.axis_index("section")
    every_id = lax.all_gather(token_ids, "fsdp", axis=0, tiled=True)
    shifted = jnp.roll(every_id, -1)
    looked = jnp.take(table, shifted, axis=1)
    embed_block = lax.all_to_all(looked, "fsdp", split_axis=1, concat_axis=0, tiled=True)
    hidden_f = hidden.astype(jnp.float32)
    embed_f = embed_block.astype(jnp.float32)
    hidden_sq, embed_sq = lax.psum(
        (jnp.sum(hidden_f * hidden_f, axis=1), jnp.sum(embed_f * embed_f, axis=0)), "section"
    )
    hidden_scale = lax.rsqrt(hidden_sq / model_width + EPS)
    embed_scale = lax.rsqrt(embed_sq / model_width + EPS)
    gain_h = lax.dynamic_slice_in_dim(gain_hidden, section_pos * block_width, block_width)
    gain_e = lax.dynamic_slice_in_dim(gain_embed, section_pos * block_width, block_width)
    hidden_norm = (hidden_f * hidden_scale[:, None] * gain_h[None, :]).astype(jnp.bfloat16)
    embed_norm = (embed_f * embed_scale[None, :] * gain_e[:, None]).astype(jnp.bfloat16)
    hidden_panel, embed_panel = (
        lax.all_to_all(proj_hidden, "section", split_axis=1, concat_axis=0, tiled=True),
        lax.all_to_all(proj_embed, "section", split_axis=1, concat_axis=0, tiled=True),
    )
    hidden_all, embed_all = (
        lax.all_gather(hidden_norm, "section", axis=1, tiled=True),
        lax.all_gather(embed_norm, "section", axis=0, tiled=True),
    )
    hidden_split = hidden_all.reshape(tokens_here, sections, groups, shard_rows)
    embed_split = embed_all.reshape(sections, groups, shard_rows, tokens_here)
    pieces = (
        lax.all_gather(hidden_panel, "fsdp", axis=0, tiled=True),
        lax.all_gather(embed_panel, "fsdp", axis=0, tiled=True),
    )
    count = pieces[0].shape[0]
    left = hidden_split
    left = left.transpose(0, 2, 1, 3).reshape(tokens_here, count)
    right = embed_split
    right = right.transpose(1, 0, 2, 3).reshape(count, tokens_here)
    left, right = (left, right)
    total = jnp.dot(left, pieces[0], preferred_element_type=jnp.float32)
    mixed = total + lax.dot_general(
        right, pieces[1], (((0,), (0,)), ((), ())), preferred_element_type=jnp.float32
    )
    return mixed.astype(jnp.bfloat16)


def solution(mesh):
    placed = (
        P("fsdp", "section"),
        P("fsdp"),
        P(("section", "fsdp"), None),
        P(),
        P(),
        P(("section", "fsdp"), None),
        P(("section", "fsdp"), None),
    )
    return jax.shard_map(
        on_device, mesh=mesh, in_specs=placed, out_specs=P("fsdp", "section"), check_vma=False
    )
```

profile of v0, /device:TPU:1, one launch (start us, length us, event | category | flops | bytes accessed | tf_op | source)
XLA Modules:
  0.0 526.5 jit_solution(9763572431352885462)
XLA Ops:
  6.5 49.0 %all-gather = s32[32,1,512]{2,1,0:T(1,128)S(1)} all-gather(s32[1,1,512]{2,1,0:T(1,128)} %bitcast.41), channel_id=1, replica_groups=mesh['section'=8,'fsdp'=32] {'fsdp'}, dimensions={0}, use_global_device_ids=true | all-gather | bytes 67584 | tf_op jit(solution)/shard_map/all_gather | solution.py:17
  55.5 0.5 slice.13
  56.1 0.1 slice.12
  56.1 13.9 %copy.19 = bf16[28,65536]{0,1:T(8,128)(2,1)} copy(bf16[28,65536]{1,0:T(8,128)(2,1)} %param.9) | data formatting | bytes 7340032 | tf_op args[2]
  70.1 0.7 pad_add_fusion
  70.8 0.8 compare_select_fusion
  71.6 0.0 copy-start
  71.6 63.3 %gather_fusion = bf16[16384,28]{1,0:T(8,128)(2,1)} fusion(bf16[28,65536]{0,1:T(8,128)(2,1)} %copy.19, s32[16384]{0:T(1024)S(1)} %broadcast_clamp_fusion), kind=kCustom, calls=%fused_computation | custom fusion | bytes 1900544 | tf_op jit(solution)/shard_map/jit(_take)/gather | solution.py:19
  134.9 3.7 copy.20
  138.7 1.1 broadcast_select_fusion
  139.8 3.8 all-to-all-start.1
  143.6 0.0 all-gather.6.cloned.1.call-start
  143.6 0.8 dynamic_slice.6
  144.4 0.0 copy-done
  144.4 0.3 fusion.1
  144.6 0.0 copy-start.1
  144.6 26.6 %all-to-all-done.1 = bf16[28,32,512]{2,0,1:T(8,128)(2,1)S(1)} async-done(((bf16[28,32,512]{2,0,1:T(8,128)(2,1)}), bf16[28,32,512]{2,0,1:T(8,128)(2,1)S(1)}, u32[]{:S(2)}, u32[]{:S(2)}) %all-to-all-start.1) | async-done | bytes 917536 | tf_op jit(solution)/shard_map/all_to_all | solution.py:20
  171.2 0.3 fusion
  171.5 17.1 %all-reduce = (f32[512]{0:T(512)S(1)}, f32[512]{0:T(512)S(1)}) all-reduce(f32[512]{0:T(512)S(1)} %fusion.1, f32[512]{0:T(512)S(1)} %fusion), channel_id=1, replica_groups=mesh['section'=8,'fsdp'=32] {'section'}, use_global_device_ids=true, to_apply=%region_1.2 | all-reduce | flops 1024 | bytes 8192 | tf_op jit(solution)/shard_map/psum | solution.py:23
  188.7 1.2 fusion.3
  189.9 0.0 all-gather.6.cloned.1.call-update
  189.9 0.0 all-gather.10.cloned.1.call-start
  189.9 0.8 dynamic_slice.7
  190.7 0.3 convert_bitcast_fusion
  191.0 1.5 reshape.130
  192.5 2.6 multiply_convert_fusion
  195.1 0.0 all-gather.10.cloned.1.call-update
  195.2 0.0 all-gather.8.cloned.1.call-start
  195.2 0.0 copy-done.1
  195.2 0.1 copy.23
  195.3 0.1 copy.18
  195.4 10.0 %all_to_all.48 = bf16[28,8,512]{2,0,1:T(8,128)(2,1)S(1)} all-to-all(bf16[28,8,512]{2,0,1:T(8,128)(2,1)S(1)} %copy.18), channel_id=1, replica_groups=mesh['section'=8,'fsdp'=32] {'section'}, dimensions={1} | all-to-all | bytes 458752 | tf_op jit(solution)/shard_map/all_to_all | solution.py:33
  205.4 0.7 all_to_all.39
  206.1 0.0 all-gather.8.cloned.1.call-update
  206.1 0.0 all-gather.12.cloned.1.call-start
  206.2 1.0 copy.24
  207.2 0.1 copy.22
  207.3 12.0 %all_to_all.49 = bf16[28,8,512]{2,0,1:T(8,128)(2,1)S(1)} all-to-all(bf16[28,8,512]{2,0,1:T(8,128)(2,1)S(1)} %copy.22), channel_id=1, replica_groups=mesh['section'=8,'fsdp'=32] {'section'}, dimensions={1} | all-to-all | bytes 458752 | tf_op jit(solution)/shard_map/all_to_all | solution.py:34
  219.4 0.7 all_to_all.44
  220.1 0.0 all-gather.12.cloned.1.call-update
  220.1 57.8 %all-gather.6.cloned.1.call-done = bf16[512,7168]{1,0:T(8,128)(2,1)} async-done(((bf16[512,896]{1,0:T(8,128)(2,1)}), bf16[512,7168]{1,0:T(8,128)(2,1)}) %all-gather.6.cloned.1.call-update) | async-done | bytes 7340048 | tf_op jit(solution)/shard_map/all_gather | solution.py:37
  278.0 10.4 %copy.16 = bf16[512,7168]{0,1:T(8,128)(2,1)} copy(bf16[512,7168]{1,0:T(8,128)(2,1)} %all-gather.6.cloned.1.call-done) | data formatting | bytes 14680064 | tf_op jit(solution)/shard_map/all_gather | solution.py:37
  288.3 11.6 %reshape.126 = bf16[512,8,32,28]{0,3,2,1:T(8,128)(2,1)} reshape(bf16[512,7168]{0,1:T(8,128)(2,1)} %copy.16) | data formatting | bytes 14680064 | tf_op jit(solution)/shard_map/reshape | solution.py:40
  299.9 8.4 %copy.17 = bf16[512,32,8,28]{0,3,2,1:T(8,128)(2,1)} copy(bf16[512,32,8,28]{0,3,1,2:T(8,128)(2,1)} %bitcast.28) | data formatting | bytes 14680064 | tf_op jit(solution)/shard_map/transpose | solution.py:48
  308.2 11.6 %reshape.127 = bf16[512,7168]{0,1:T(8,128)(2,1)} reshape(bf16[512,32,8,28]{0,3,2,1:T(8,128)(2,1)} %copy.17) | data formatting | bytes 14680064 | tf_op jit(solution)/shard_map/reshape | solution.py:48
  319.8 41.5 %all-gather.10.cloned.1.call-done = bf16[7168,512]{1,0:T(8,128)(2,1)} async-done(((bf16[896,512]{1,0:T(8,128)(2,1)}), bf16[7168,512]{1,0:T(8,128)(2,1)}) %all-gather.10.cloned.1.call-update) | async-done | bytes 7340048 | tf_op jit(solution)/shard_map/all_gather | solution.py:38
  361.3 11.5 %reshape.128 = bf16[8,32,28,512]{3,2,1,0:T(8,128)(2,1)} reshape(bf16[7168,512]{1,0:T(8,128)(2,1)} %all-gather.10.cloned.1.call-done) | data formatting | bytes 14680064 | tf_op jit(solution)/shard_map/reshape | solution.py:41
  372.8 8.5 %copy.21 = bf16[32,8,28,512]{3,2,1,0:T(8,128)(2,1)} copy(bf16[32,8,28,512]{3,2,0,1:T(8,128)(2,1)} %bitcast.29) | data formatting | bytes 14680064 | tf_op jit(solution)/shard_map/transpose | solution.py:50
  381.2 11.6 %reshape.129 = bf16[7168,512]{1,0:T(8,128)(2,1)} reshape(bf16[32,8,28,512]{3,2,1,0:T(8,128)(2,1)} %copy.21) | data formatting | bytes 14680064 | tf_op jit(solution)/shard_map/reshape | solution.py:50
  392.8 43.1 %all-gather.8.cloned.1.call-done = bf16[7168,512]{1,0:T(8,128)(2,1)} async-done(((bf16[224,512]{1,0:T(8,128)(2,1)}), bf16[7168,512]{1,0:T(8,128)(2,1)}) %all-gather.8.cloned.1.call-update) | async-done | bytes 7340048 | tf_op jit(solution)/shard_map/all_gather | solution.py:43
  435.9 8.5 %fusion.5 = f32[512,512]{1,0:T(8,128)S(1)} fusion(bf16[512,7168]{0,1:T(8,128)(2,1)} %reshape.127, bf16[7168,512]{1,0:T(8,128)(2,1)} %all-gather.8.cloned.1.call-done), kind=kOutput, calls=%fused_computation.20 | convolution fusion | flops 3758096384 | bytes 15728640 | tf_op jit(solution)/shard_map/dot_general | solution.py:52
  444.4 65.6 %all-gather.12.cloned.1.call-done = bf16[7168,512]{1,0:T(8,128)(2,1)} async-done(((bf16[224,512]{1,0:T(8,128)(2,1)}), bf16[7168,512]{1,0:T(8,128)(2,1)}) %all-gather.12.cloned.1.call-update) | async-done | bytes 7340048 | tf_op jit(solution)/shard_map/all_gather | solution.py:44
  510.0 10.0 %fusion.4 = bf16[512,512]{1,0:T(8,128)(2,1)} fusion(f32[512,512]{1,0:T(8,128)S(1)} %fusion.5, bf16[7168,512]{1,0:T(8,128)(2,1)} %reshape.129, bf16[7168,512]{1,0:T(8,128)(2,1)} %all-gather.12.cloned.1.call-done), kind=kOutput, calls=%fused_computation.11 | convolution fusion | flops 3758620672 | bytes 16252928 | tf_op jit(solution)/shard_map/dot_general | solution.py:53
  (7 shorter events, 0.1 us)
Async XLA Ops:
  71.6 72.8 %copy-start = (bf16[512,896]{1,0:T(8,128)(2,1)S(1)}, bf16[512,896]{1,0:T(8,128)(2,1)}, u32[]{:S(2)}) copy-start(bf16[512,896]{1,0:T(8,128)(2,1)} %param.7) | copy-start | bytes 2752516
  139.8 31.4 %all-to-all-start.1 = ((bf16[28,32,512]{2,0,1:T(8,128)(2,1)}), bf16[28,32,512]{2,0,1:T(8,128)(2,1)S(1)}, u32[]{:S(2)}, u32[]{:S(2)}) async-start(bf16[28,32,512]{2,0,1:T(8,128)(2,1)} %broadcast_select_fusion), calls=%async_computation.1 | async-start | bytes 2097152 | tf_op jit(solution)/shard_map/all_to_all | solution.py:20
  143.6 134.4 %all-gather.6.cloned.1.call-start = ((), (), s32[]{:S(2)}) async-start(), calls=%async_computation.3 | async-start | bytes 8257536 | tf_op jit(solution)/shard_map/all_gather | solution.py:37
  144.6 50.6 %copy-start.1 = (bf16[28,4096]{1,0:T(8,128)(2,1)S(1)}, bf16[28,4096]{1,0:T(8,128)(2,1)}, u32[]{:S(2)}) copy-start(bf16[28,4096]{1,0:T(8,128)(2,1)} %param.12) | copy-start | bytes 688132
  189.9 171.4 %all-gather.10.cloned.1.call-start = ((), (), s32[]{:S(2)}) async-start(), calls=%async_computation.5 | async-start | bytes 8257536 | tf_op jit(solution)/shard_map/all_gather | solution.py:38
  195.2 240.7 %all-gather.8.cloned.1.call-start = ((), (), s32[]{:S(2)}) async-start(), calls=%async_computation.4 | async-start | bytes 7569408 | tf_op jit(solution)/shard_map/all_gather | solution.py:43
  206.1 303.9 %all-gather.12.cloned.1.call-start = ((), (), s32[]{:S(2)}) async-start(), calls=%async_computation.6 | async-start | bytes 7569408 | tf_op jit(solution)/shard_map/all_gather | solution.py:44
Sparse Core Ops, SparseCore 0:
  190.0 87.8 all-gather.5
  279.7 81.4 all-gather.9
  363.8 72.0 all-gather.7
  438.3 71.6 all-gather.11
where the time goes:
time: 529 us; the launch traced here: 527 us
  waiting for transfers between devices  235 us (44%)
  local copies, waits for them, and re-layouts  161 us (30%)
  blocking collectives  88.1 us (17%)
  matrix products  18.5 us (3%)
  between operations  13.3 us (3%)
  other arithmetic  7.31 us (1%)
    gather x2, local copies, waits for them, and re-layouts, on_device(): looked = jnp.take(table, shifted, axis=1)  67 us
    all_gather x1, waiting for transfers between devices, on_device(): lax.all_gather(embed_panel, 'fsdp', axis=0, tiled=True)  65.6 us
    all_gather x1, waiting for transfers between devices, on_device(): lax.all_gather(hidden_norm, 'section', axis=1, tiled=True)  57.8 us
    all_gather x1, blocking collectives, on_device(): every_id = lax.all_gather(token_ids, 'fsdp', axis=0, tiled=True)  49 us
    all_gather x1, waiting for transfers between devices, on_device(): lax.all_gather(hidden_panel, 'fsdp', axis=0, tiled=True)  43.1 us
    all_gather x1, waiting for transfers between devices, on_device(): lax.all_gather(embed_norm, 'section', axis=0, tiled=True)  41.5 us
    all_to_all x1, waiting for transfers between devices, on_device(): lax.all_to_all(looked, 'fsdp', split_axis=1, concat_axis=0, tiled=True)  26.6 us
    psum x1, blocking collectives, on_device(): lax.psum((jnp.sum(hidden_f * hidden_f, axis=1), jnp.sum(embed_f * embed_f...  17.1 us
  transfers between devices with their start and end apart: 5, of which 5 were waited for; matrix products, arithmetic and copies ran while one was open for 17% of the time, Pallas kernels for 0%

commit v1 on v0

--- a/solution.py
+++ b/solution.py
@@ -17,7 +17,10 @@
     every_id = lax.all_gather(token_ids, "fsdp", axis=0, tiled=True)
     shifted = jnp.roll(every_id, -1)
     looked = jnp.take(table, shifted, axis=1)
-    embed_block = lax.all_to_all(looked, "fsdp", split_axis=1, concat_axis=0, tiled=True)
+    embed_block = jnp.concatenate(
+        lax.all_to_all(jnp.stack(jnp.split(looked, lax.axis_size("fsdp"), axis=1)), "fsdp", 0, 0),
+        axis=0,
+    )
     hidden_f = hidden.astype(jnp.float32)
     embed_f = embed_block.astype(jnp.float32)
     hidden_sq, embed_sq = lax.psum(

time: 529 us -> 559 us (1.057)
  local copies, waits for them, and re-layouts: 161 us -> 180 us
  other arithmetic: 7.31 us -> 15.4 us
    unnamed x7 -> x40, local copies, waits for them, and re-layouts: 15 us -> 34.5 us
    select_n x2, other arithmetic: 1.88 us -> 11.7 us  [on_device(): looked = jnp.take(table, shifted, axis=1)]
    gather x2 -> x1, local copies, waits for them, and re-layouts: 67 us -> 62.9 us  [on_device(): looked = jnp.take(table, shifted, axis=1)]
  transfers between devices with their start and end apart: 5 -> 5, of which waited for: 5 -> 5; matrix products, arithmetic and copies ran while one was open for 17% -> 15% of each run, Pallas kernels for 0% -> 0%
where the time goes in v1:
time: 559 us; the launch traced here: 557 us
  waiting for transfers between devices  240 us (43%)
  local copies, waits for them, and re-layouts  180 us (32%)
  blocking collectives  86.3 us (15%)
  matrix products  18.5 us (3%)
  other arithmetic  15.4 us (3%)
  between operations  13.3 us (2%)
    all_gather x1, waiting for transfers between devices, on_device(): lax.all_gather(embed_panel, 'fsdp', axis=0, tiled=True)  65.6 us
    gather x1, local copies, waits for them, and re-layouts, on_device(): looked = jnp.take(table, shifted, axis=1)  62.9 us
    all_gather x1, waiting for transfers between devices, on_device(): lax.all_gather(hidden_norm, 'section', axis=1, tiled=True)  62.4 us
    all_gather x1, blocking collectives, on_device(): every_id = lax.all_gather(token_ids, 'fsdp', axis=0, tiled=True)  49 us
    all_gather x1, waiting for transfers between devices, on_device(): lax.all_gather(hidden_panel, 'fsdp', axis=0, tiled=True)  43.1 us
    all_gather x1, waiting for transfers between devices, on_device(): lax.all_gather(embed_norm, 'section', axis=0, tiled=True)  41.8 us
    unnamed x40, local copies, waits for them, and re-layouts  34.5 us
    all_to_all x1, waiting for transfers between devices, on_device(): lax.all_to_all(jnp.stack(jnp.split(looked, lax.axis_size('fsdp'), axis=1)...  26.6 us
  transfers between devices with their start and end apart: 5, of which 5 were waited for; matrix products, arithmetic and copies ran while one was open for 15% of the time, Pallas kernels for 0%

profile of v1, /device:TPU:1, one launch (start us, length us, event | category | flops | bytes accessed | tf_op | source)
XLA Modules:
  0.0 557.1 jit_solution(5061647201506427198)
XLA Ops:
  6.5 49.0 %all-gather = s32[32,1,512]{2,1,0:T(1,128)S(1)} all-gather(s32[1,1,512]{2,1,0:T(1,128)} %bitcast.165), channel_id=1, replica_groups=mesh['section'=8,'fsdp'=32] {'fsdp'}, dimensions={0}, use_global_device_ids=true | all-gather | bytes 67584 | tf_op jit(solution)/shard_map/all_gather | solution.py:17
  55.5 0.5 slice.13
  56.1 13.9 %copy.58 = bf16[28,65536]{0,1:T(8,128)(2,1)} copy(bf16[28,65536]{1,0:T(8,128)(2,1)} %param.9) | data formatting | bytes 7340032 | tf_op args[2]
  70.0 0.7 compare_and_fusion
  70.8 0.8 compare_select_fusion
  71.6 62.9 %gather_fusion = bf16[16384,28]{1,0:T(8,128)(2,1)} fusion(bf16[28,65536]{0,1:T(8,128)(2,1)} %copy.58, s32[16384]{0:T(1024)S(1)} %broadcast_clamp_fusion), kind=kCustom, calls=%fused_computation | custom fusion | bytes 1900544 | tf_op jit(solution)/shard_map/jit(_take)/gather | solution.py:19
  134.5 10.9 %select_bitcast_fusion = bf16[28,16384]{0,1:T(8,128)(2,1)S(1)} fusion(bf16[16384,28]{1,0:T(8,128)(2,1)} %gather_fusion, pred[16384]{0:T(1024)(128)(4,1)S(1)} %compare_and_fusion), kind=kLoop, calls=%fused_computation.1 | loop fusion | flops 458752 | bytes 1851392 | tf_op jit(solution)/shard_map/jit(_take)/select_n | solution.py:19
  145.4 0.7 fusion.35
  146.1 0.7 fusion.34
  146.7 0.6 fusion.33
  147.4 0.7 fusion.32
  148.0 0.7 fusion.31
  148.7 0.7 fusion.30
  149.3 0.7 fusion.29
  150.0 0.7 fusion.28
  150.7 0.7 fusion.27
  151.3 0.7 fusion.26
  152.0 0.7 fusion.25
  152.6 0.7 fusion.24
  153.3 0.7 fusion.23
  154.0 0.7 fusion.22
  154.6 0.6 fusion.21
  155.3 0.7 fusion.20
  155.9 0.7 fusion.19
  156.6 0.7 fusion.18
  157.3 0.7 fusion.17
  157.9 0.7 fusion.16
  158.6 0.7 fusion.15
  159.3 0.7 fusion.14
  159.9 0.7 fusion.13
  160.6 0.7 fusion.12
  161.2 0.7 fusion.11
  161.9 0.7 fusion.10
  162.6 0.6 fusion.9
  163.2 0.6 fusion.8
  163.9 0.7 fusion.7
  164.5 0.7 fusion.6
  165.2 0.6 fusion.5
  165.8 0.6 fusion.4
  166.5 4.7 copy.59
  171.2 3.8 all-to-all-start.1
  175.0 0.8 dynamic_slice.6
  176.0 26.6 %all-to-all-done.1 = bf16[32,28,512]{2,1,0:T(8,128)(2,1)S(1)} async-done(((bf16[32,28,512]{2,1,0:T(8,128)(2,1)}), bf16[32,28,512]{2,1,0:T(8,128)(2,1)S(1)}, u32[]{:S(2)}, u32[]{:S(2)}) %all-to-all-start.1) | async-done | bytes 917536 | tf_op jit(solution)/shard_map/all_to_all | solution.py:21
  202.9 17.1 %all-reduce = (f32[512]{0:T(512)S(1)}, f32[512]{0:T(512)S(1)}) all-reduce(f32[512]{0:T(512)S(1)} %fusion, f32[512]{0:T(512)S(1)} %multiply_reduce_fusion), channel_id=1, replica_groups=mesh['section'=8,'fsdp'=32] {'section'}, use_global_device_ids=true, to_apply=%region_1.2 | all-reduce | flops 1024 | bytes 8192 | tf_op jit(solution)/shard_map/psum | solution.py:26
  220.0 1.2 fusion.2
  221.3 0.8 dynamic_slice.7
  222.3 1.1 multiply_convert_fusion
  223.7 8.5 %all_to_all.43 = bf16[28,8,512]{2,0,1:T(8,128)(2,1)S(1)} all-to-all(bf16[28,8,512]{2,0,1:T(8,128)(2,1)S(1)} %copy.57), channel_id=1, replica_groups=mesh['section'=8,'fsdp'=32] {'section'}, dimensions={1} | all-to-all | bytes 458752 | tf_op jit(solution)/shard_map/all_to_all | solution.py:36
  232.2 0.7 all_to_all.34
  233.2 11.7 %all_to_all.44 = bf16[28,8,512]{2,0,1:T(8,128)(2,1)S(1)} all-to-all(bf16[28,8,512]{2,0,1:T(8,128)(2,1)S(1)} %copy.61), channel_id=1, replica_groups=mesh['section'=8,'fsdp'=32] {'section'}, dimensions={1} | all-to-all | bytes 458752 | tf_op jit(solution)/shard_map/all_to_all | solution.py:37
  244.9 0.7 all_to_all.39
  245.7 62.4 %all-gather.6.cloned.1.call-done = bf16[512,7168]{1,0:T(8,128)(2,1)} async-done(((bf16[512,896]{1,0:T(8,128)(2,1)}), bf16[512,7168]{1,0:T(8,128)(2,1)}) %all-gather.6.cloned.1.call-update) | async-done | bytes 7340048 | tf_op jit(solution)/shard_map/all_gather | solution.py:40
  308.1 10.4 %copy.55 = bf16[512,7168]{0,1:T(8,128)(2,1)} copy(bf16[512,7168]{1,0:T(8,128)(2,1)} %all-gather.6.cloned.1.call-done) | data formatting | bytes 14680064 | tf_op jit(solution)/shard_map/all_gather | solution.py:40
  318.5 11.6 %reshape.118 = bf16[512,8,32,28]{0,3,2,1:T(8,128)(2,1)} reshape(bf16[512,7168]{0,1:T(8,128)(2,1)} %copy.55) | data formatting | bytes 14680064 | tf_op jit(solution)/shard_map/reshape | solution.py:43
  330.1 8.4 %copy.56 = bf16[512,32,8,28]{0,3,2,1:T(8,128)(2,1)} copy(bf16[512,32,8,28]{0,3,1,2:T(8,128)(2,1)} %bitcast.153) | data formatting | bytes 14680064 | tf_op jit(solution)/shard_map/transpose | solution.py:51
  338.5 11.6 %reshape.119 = bf16[512,7168]{0,1:T(8,128)(2,1)} reshape(bf16[512,32,8,28]{0,3,2,1:T(8,128)(2,1)} %copy.56) | data formatting | bytes 14680064 | tf_op jit(solution)/shard_map/reshape | solution.py:51
  350.0 41.8 %all-gather.10.cloned.1.call-done = bf16[7168,512]{1,0:T(8,128)(2,1)} async-done(((bf16[896,512]{1,0:T(8,128)(2,1)}), bf16[7168,512]{1,0:T(8,128)(2,1)}) %all-gather.10.cloned.1.call-update) | async-done | bytes 7340048 | tf_op jit(solution)/shard_map/all_gather | solution.py:41
  391.8 11.5 %reshape.120 = bf16[8,32,28,512]{3,2,1,0:T(8,128)(2,1)} reshape(bf16[7168,512]{1,0:T(8,128)(2,1)} %all-gather.10.cloned.1.call-done) | data formatting | bytes 14680064 | tf_op jit(solution)/shard_map/reshape | solution.py:44
  403.3 8.4 %copy.60 = bf16[32,8,28,512]{3,2,1,0:T(8,128)(2,1)} copy(bf16[32,8,28,512]{3,2,0,1:T(8,128)(2,1)} %bitcast.154) | data formatting | bytes 14680064 | tf_op jit(solution)/shard_map/transpose | solution.py:53
  411.8 11.6 %reshape.121 = bf16[7168,512]{1,0:T(8,128)(2,1)} reshape(bf16[32,8,28,512]{3,2,1,0:T(8,128)(2,1)} %copy.60) | data formatting | bytes 14680064 | tf_op jit(solution)/shard_map/reshape | solution.py:53
  423.3 43.1 %all-gather.8.cloned.1.call-done = bf16[7168,512]{1,0:T(8,128)(2,1)} async-done(((bf16[224,512]{1,0:T(8,128)(2,1)}), bf16[7168,512]{1,0:T(8,128)(2,1)}) %all-gather.8.cloned.1.call-update) | async-done | bytes 7340048 | tf_op jit(solution)/shard_map/all_gather | solution.py:46
  466.4 8.5 %fusion.36 = f32[512,512]{1,0:T(8,128)S(1)} fusion(bf16[512,7168]{0,1:T(8,128)(2,1)} %reshape.119, bf16[7168,512]{1,0:T(8,128)(2,1)} %all-gather.8.cloned.1.call-done), kind=kOutput, calls=%fused_computation.81 | convolution fusion | flops 3758096384 | bytes 15728640 | tf_op jit(solution)/shard_map/dot_general | solution.py:55
  474.9 65.6 %all-gather.12.cloned.1.call-done = bf16[7168,512]{1,0:T(8,128)(2,1)} async-done(((bf16[224,512]{1,0:T(8,128)(2,1)}), bf16[7168,512]{1,0:T(8,128)(2,1)}) %all-gather.12.cloned.1.call-update) | async-done | bytes 7340048 | tf_op jit(solution)/shard_map/all_gather | solution.py:47
  540.5 10.0 %fusion.3 = bf16[512,512]{1,0:T(8,128)(2,1)} fusion(f32[512,512]{1,0:T(8,128)S(1)} %fusion.36, bf16[7168,512]{1,0:T(8,128)(2,1)} %reshape.121, bf16[7168,512]{1,0:T(8,128)(2,1)} %all-gather.12.cloned.1.call-done), kind=kOutput, calls=%fused_computation.10 | convolution fusion | flops 3758620672 | bytes 16252928 | tf_op jit(solution)/shard_map/dot_general | solution.py:56
  (27 shorter events, 1.4 us)
Async XLA Ops:
  163.9 11.9 %copy-start = (bf16[512,896]{1,0:T(8,128)(2,1)S(1)}, bf16[512,896]{1,0:T(8,128)(2,1)}, u32[]{:S(2)}) copy-start(bf16[512,896]{1,0:T(8,128)(2,1)} %param.7) | copy-start | bytes 2752516
  171.2 31.4 %all-to-all-start.1 = ((bf16[32,28,512]{2,1,0:T(8,128)(2,1)}), bf16[32,28,512]{2,1,0:T(8,128)(2,1)S(1)}, u32[]{:S(2)}, u32[]{:S(2)}) async-start(bf16[32,28,512]{2,1,0:T(8,128)(2,1)} %copy.59), calls=%async_computation.1 | async-start | bytes 2097152 | tf_op jit(solution)/shard_map/all_to_all | solution.py:21
  174.9 133.2 %all-gather.6.cloned.1.call-start = ((), (), s32[]{:S(2)}) async-start(), calls=%async_computation.3 | async-start | bytes 8257536 | tf_op jit(solution)/shard_map/all_gather | solution.py:40
  221.2 2.3 copy-start.1
  221.3 170.5 %all-gather.10.cloned.1.call-start = ((), (), s32[]{:S(2)}) async-start(), calls=%async_computation.5 | async-start | bytes 8257536 | tf_op jit(solution)/shard_map/all_gather | solution.py:41
  222.1 10.9 %copy-start.2 = (bf16[28,4096]{1,0:T(8,128)(2,1)S(1)}, bf16[28,4096]{1,0:T(8,128)(2,1)}, u32[]{:S(2)}) copy-start(bf16[28,4096]{1,0:T(8,128)(2,1)} %param.13) | copy-start | bytes 688132
  223.5 243.0 %all-gather.8.cloned.1.call-start = ((), (), s32[]{:S(2)}) async-start(), calls=%async_computation.4 | async-start | bytes 7569408 | tf_op jit(solution)/shard_map/all_gather | solution.py:46
  233.0 307.6 %all-gather.12.cloned.1.call-start = ((), (), s32[]{:S(2)}) async-start(), calls=%async_computation.6 | async-start | bytes 7569408 | tf_op jit(solution)/shard_map/all_gather | solution.py:47
Sparse Core Ops, SparseCore 0:
  221.4 86.6 all-gather.5
  309.9 81.8 all-gather.9
  394.3 72.0 all-gather.7
  468.8 71.6 all-gather.11
